TPU v7x, 32 devices: a whole 2x2x4 slice. The times are simulated.
32 devices in a mesh: dp: 16 (over z, x, core), seq: 2 (over y).
Axes of the slice: x: 2, y: 2, z: 4, core: 2. Of those that a mesh axis runs over, the one named last changes fastest.
Arguments:
- queries: bfloat16 [4096, 4096], P(('dp', 'seq')), may hold values from -6 to 6
- keys: bfloat16 [4096, 512], P(('dp', 'seq')), may hold values from -6 to 6
- values: bfloat16 [4096, 512], P(('dp', 'seq')), may hold values from -6 to 6
- grad_out: bfloat16 [4096, 4096], P(('dp', 'seq')), may hold values from -6 to 6
- quant_scale: float32 [2, 4, 128], replicated, may hold values from 2 to 8
- doc_lengths: int32 [16, 8], P('dp'), may hold values from 1 to 128, as said below
Outputs:
- attn_out: bfloat16 [4096, 4096], P(('dp', 'seq'))
- grad_queries: bfloat16 [4096, 4096], P(('dp', 'seq'))
- grad_keys: bfloat16 [4096, 512], P(('dp', 'seq'))
- grad_values: bfloat16 [4096, 512], P(('dp', 'seq'))
- grad_scale: float32 [2, 4, 128], replicated
Inputs may be any that keep to these rules, and one draw needn't show every extreme that they name: `doc_lengths`: each row sums to 256; its largest length is exactly 128.
All inputs are finite; a program needn't handle non-finite values.
Results may differ from a plain program's by a relative error of at most 0.04.
Values may be sent and summed in bfloat16 or wider, within the bound.
No kernel may reach another device: no remote copies, remote signals or barrier semaphores. Data moves between devices by JAX's collectives and lax.ppermute only.
A program may use at most 64 MiB of HBM per device.

v0:
```python
import functools
import math

import jax
import jax.numpy as jnp
from jax import lax
from jax.experimental import pallas as pl
from jax.experimental.pallas import tpu as pltpu
from jax.sharding import PartitionSpec as P

F32 = jnp.float32
BF16 = jnp.bfloat16
LEVELS = 127.0
NEG = -1e30


def sin_cos_half(u):
    r = (u - jnp.round(u)) * math.pi
    z = r * r
    s = z * (1.0 / 6227020800.0) - 1.0 / 39916800.0
    for c in (1.0 / 362880.0, -1.0 / 5040.0, 1.0 / 120.0, -1.0 / 6.0, 1.0):
        s = s * z + c
    s = s * r
    k = z * (1.0 / 479001600.0) - 1.0 / 3628800.0
    for c in (1.0 / 40320.0, -1.0 / 720.0, 1.0 / 24.0, -0.5, 1.0):
        k = k * z + c
    return s, k


def quant_parts(x, clip):
    inv = 1.0 / clip
    ratio = x * inv
    t = jnp.tanh(ratio)
    u = LEVELS * t
    s, k = sin_cos_half(u)
    level = u - s * k * (1.0 / math.pi)
    unit = level * (1.0 / LEVELS)
    slope = (2.0 * s * s) * (1.0 - t * t)
    return clip * unit, slope, unit - slope * ratio


def prep_kernel(nb, q_hbm, g_hbm, key_hbm, value_hbm, clip_hbm, len_hbm, q_ref, g_ref, quant_ref, slope_ref,
                dclip_ref, bias_ref, clip_out, key_ref, value_ref, len_ref, sems):
    small = [
        pltpu.make_async_copy(src, dst, sems.at[i])
        for i, (src, dst) in enumerate(
            ((len_hbm, len_ref), (clip_hbm, clip_out), (key_hbm, key_ref), (value_hbm, value_ref))
        )
    ]
    large = [
        pltpu.make_async_copy(q_hbm, q_ref, sems.at[4]),
        pltpu.make_async_copy(g_hbm, g_ref, sems.at[5]),
    ]
    for copy in small + large:
        copy.start()
    rows = key_ref.shape[0]
    kv_heads, hd = clip_out.shape[1], clip_out.shape[2]
    base = lax.axis_index("seq") * rows
    for copy in small:
        copy.wait()
    for side, src in ((0, key_ref), (1, value_ref)):
        for n in range(kv_heads):
            x = src[:, n * hd:(n + 1) * hd].astype(F32)
            q, slope, dclip = quant_parts(x, clip_out[side, n:n + 1, :])
            at = slice((side * kv_heads + n) * hd, (side * kv_heads + n + 1) * hd)
            quant_ref[:, at] = q.astype(BF16)
            slope_ref[:, at] = slope
            dclip_ref[:, at] = dclip
    row = lax.broadcasted_iota(jnp.int32, (rows, rows), 0)
    col = lax.broadcasted_iota(jnp.int32, (rows, rows), 1)
    start = jnp.zeros((rows, rows), jnp.int32)
    end = jnp.int32(0)
    for d in range(len_ref.shape[1]):
        end = end + len_ref[0, d]
        start = jnp.where(row + base >= end, end, start)
    for b in range(nb):
        if b == 0:
            pos = jnp.where(col <= row, col, col - nb * rows)
        else:
            pos = col - b * rows
        bias_ref[:, b * rows:(b + 1) * rows] = jnp.where(pos + base >= start, 0.0, NEG)
    for copy in large:
        copy.wait()


def attend_kernel(nb, q_ref, g_ref, quant_ref, dclip_ref, bias_ref, clip_ref, *rest):
    far_k, far_v = rest[:nb], rest[nb:2 * nb]
    out_hbm, gq_hbm, grad_ref, far_ref, spread_ref, out_ref, gq_ref, scale_ref, sems = rest[2 * nb:]
    kv_heads, hd = clip_ref.shape[1], clip_ref.shape[2]
    rows, group = q_ref.shape[0], q_ref.shape[1] // kv_heads
    heads = group // hd
    width = kv_heads * hd
    scale = hd ** -0.5
    log2e = math.log2(math.e)
    across = (((1,), (1,)), ((), ()))
    down = (((0,), (0,)), ((), ()))
    row = lax.broadcasted_iota(jnp.int32, (rows, rows), 0)
    col = lax.broadcasted_iota(jnp.int32, (rows, rows), 1)
    near = col <= row
    near_b = near.astype(F32).astype(BF16)
    far_b = 1.0 - near_b

    def merge(x):
        first = jnp.where(near, x[:, :rows], x[:, rows:2 * rows])
        return jnp.concatenate([first, x[:, 2 * rows:]], axis=1) if nb > 1 else first

    def split(x):
        first = x[:, :rows]
        parts = [first * near_b, first * far_b]
        if nb > 1:
            parts.append(x[:, rows:])
        return jnp.concatenate(parts, axis=1)

    def copies(n):
        cols = pl.ds(pl.multiple_of(n * group, group), group)
        return (
            pltpu.make_async_copy(out_ref.at[:, cols], out_hbm.at[:, cols], sems.at[0, n]),
            pltpu.make_async_copy(gq_ref.at[:, cols], gq_hbm.at[:, cols], sems.at[1, n]),
        )

    def step(n, carry):
        k_cols = pl.ds(pl.multiple_of(n * hd, hd), hd)
        v_cols = pl.ds(pl.multiple_of(width + n * hd, hd), hd)
        k_clip = clip_ref[0, pl.ds(n, 1), :]
        v_clip = clip_ref[1, pl.ds(n, 1), :]
        ks, vs = [quant_ref[:, k_cols]], [quant_ref[:, v_cols]]
        kd, vd = [dclip_ref[:, k_cols]], [dclip_ref[:, v_cols]]
        for d in [nb] + list(range(1, nb)):
            q, _, dc = quant_parts(far_k[d - 1][:, k_cols].astype(F32), k_clip)
            ks.append(q.astype(BF16))
            kd.append(dc)
            q, _, dc = quant_parts(far_v[d - 1][:, k_cols].astype(F32), v_clip)
            vs.append(q.astype(BF16))
            vd.append(dc)
        k2 = jnp.concatenate(ks, axis=0)
        v2 = jnp.concatenate(vs, axis=0)

        def head_cols(h):
            return pl.ds(pl.multiple_of(n * group + h * hd, hd), hd)

        qs = jnp.concatenate([q_ref[:, head_cols(h)] for h in range(heads)], axis=0)
        gs = jnp.concatenate([g_ref[:, head_cols(h)] for h in range(heads)], axis=0)
        s_all = lax.dot_general(qs, k2, across, preferred_element_type=F32)
        d_all = lax.dot_general(gs, v2, across, preferred_element_type=F32)
        bias = bias_ref[...]
        ps, ds = [], []
        for h in range(heads):
            at = slice(h * rows, (h + 1) * rows)
            s = merge(s_all[at]) * (scale * log2e) + bias
            dp = merge(d_all[at])
            w = jnp.exp2(s - jnp.max(s, axis=1, keepdims=True))
            inv = 1.0 / jnp.sum(w, axis=1, keepdims=True)
            p = w * inv
            delta = jnp.sum(p * dp, axis=1, keepdims=True)
            p2 = split(p.astype(BF16))
            ds2 = split((p * ((dp - delta) * scale)).astype(BF16))
            out_ref[:, head_cols(h)] = jnp.dot(p2, v2, preferred_element_type=F32).astype(BF16)
            gq_ref[:, head_cols(h)] = jnp.dot(ds2, k2, preferred_element_type=F32).astype(BF16)
            ps.append(p2)
            ds.append(ds2)
        for copy in copies(n):
            copy.start()
        k_grad = lax.dot_general(qs, jnp.concatenate(ds, axis=0), down, preferred_element_type=F32).T
        v_grad = lax.dot_general(gs, jnp.concatenate(ps, axis=0), down, preferred_element_type=F32).T
        grad_ref[:, k_cols] = k_grad[:rows]
        grad_ref[:, v_cols] = v_grad[:rows]
        far_ref[:, k_cols] = k_grad[rows:].astype(BF16)
        far_ref[:, v_cols] = v_grad[rows:].astype(BF16)
        scale_ref[pl.ds(n, 1), :] = jnp.sum(k_grad * jnp.concatenate(kd, axis=0), axis=0, keepdims=True)
        scale_ref[pl.ds(kv_heads + n, 1), :] = jnp.sum(
            v_grad * jnp.concatenate(vd, axis=0), axis=0, keepdims=True
        )
        return carry

    lax.fori_loop(0, kv_heads, step, 0)
    part = scale_ref[...]

    def spread(i, carry):
        spread_ref[i] = part
        return carry

    lax.fori_loop(0, spread_ref.shape[0], spread, 0)
    for n in range(kv_heads):
        for copy in copies(n):
            copy.wait()


def finish_kernel(nb, grad_ref, slope_ref, *rest):
    backs, (gk_ref, gv_ref) = rest[:nb], rest[nb:]
    width = gk_ref.shape[1]
    for side, out in ((0, gk_ref), (1, gv_ref)):
        at = slice(side * width, (side + 1) * width)
        total = grad_ref[:, at]
        for back in backs:
            total = total + back[:, at].astype(F32)
        out[...] = (total * slope_ref[:, at]).astype(BF16)


def on_device(sizes, queries, keys, values, grad_out, quant_scale, doc_lengths):
    dp_count, seq_count = sizes
    count = dp_count * seq_count
    nb = max(1, seq_count // 2)
    rows, width = keys.shape
    kv_heads, hd = quant_scale.shape[1], quant_scale.shape[2]
    vmem = pl.BlockSpec(memory_space=pltpu.VMEM)
    hbm = pl.BlockSpec(memory_space=pltpu.HBM)
    params = pltpu.CompilerParams(vmem_limit_bytes=40 * 1024 * 1024)
    shape = jax.ShapeDtypeStruct

    def shift(array, d):
        return lax.ppermute(array, "seq", [(r, r + d) for r in range(seq_count - d)])

    def unshift(array, d):
        return lax.ppermute(array, "seq", [(r + d, r) for r in range(seq_count - d)])

    far_k = [shift(keys, d) for d in range(1, nb + 1)]
    far_v = [shift(values, d) for d in range(1, nb + 1)]

    q_near, g_near, quants, slopes, dclips, bias, clips = pl.pallas_call(
        functools.partial(prep_kernel, nb),
        out_shape=(
            shape(queries.shape, BF16),
            shape(queries.shape, BF16),
            shape((rows, 2 * width), BF16),
            shape((rows, 2 * width), F32),
            shape((rows, 2 * width), F32),
            shape((rows, nb * rows), F32),
            shape(quant_scale.shape, F32),
        ),
        in_specs=[hbm] * 6,
        out_specs=(vmem,) * 7,
        scratch_shapes=[
            pltpu.VMEM(keys.shape, BF16),
            pltpu.VMEM(values.shape, BF16),
            pltpu.SMEM(doc_lengths.shape, jnp.int32),
            pltpu.SemaphoreType.DMA((6,)),
        ],
        compiler_params=params,
        cost_estimate=pl.CostEstimate(
            flops=100 * rows * width, bytes_accessed=16 * rows * width, transcendentals=2 * rows * width
        ),
        name="prep",
    )(*[pltpu.with_memory_space_constraint(x, pltpu.HBM) for x in (queries, grad_out, keys, values, quant_scale, doc_lengths)])

    attn_out, grad_queries, grads, far_grads, spread = pl.pallas_call(
        functools.partial(attend_kernel, nb),
        out_shape=(
            shape(queries.shape, BF16),
            shape(queries.shape, BF16),
            shape((rows, 2 * width), F32),
            shape((nb * rows, 2 * width), BF16),
            shape((count, 2 * kv_heads, hd), F32),
        ),
        in_specs=[vmem] * (6 + 2 * nb),
        out_specs=(hbm, hbm, vmem, vmem, vmem),
        scratch_shapes=[
            pltpu.VMEM(queries.shape, BF16),
            pltpu.VMEM(queries.shape, BF16),
            pltpu.VMEM((2 * kv_heads, hd), F32),
            pltpu.SemaphoreType.DMA((2, kv_heads)),
        ],
        compiler_params=params,
        cost_estimate=pl.CostEstimate(
            flops=12 * rows * (nb + 1) * rows * queries.shape[1],
            bytes_accessed=8 * rows * queries.shape[1],
            transcendentals=rows * rows * nb * queries.shape[1] // hd,
        ),
        name="attend",
    )(q_near, g_near, quants, dclips, bias, clips, *far_k, *far_v)

    order = [nb] + list(range(1, nb))
    backs = []
    for d in range(1, nb + 1):
        at = order.index(d) * rows
        backs.append(unshift(lax.slice_in_dim(far_grads, at, at + rows, axis=0), d))
    gathered = lax.all_to_all(spread, ("dp", "seq"), split_axis=0, concat_axis=0, tiled=True)
    grad_scale = jnp.sum(gathered, axis=0).reshape(quant_scale.shape)

    grad_keys, grad_values = pl.pallas_call(
        functools.partial(finish_kernel, nb),
        out_shape=(shape((rows, width), BF16), shape((rows, width), BF16)),
        in_specs=[vmem] * (2 + nb),
        out_specs=(vmem, vmem),
        compiler_params=params,
        cost_estimate=pl.CostEstimate(
            flops=6 * rows * width, bytes_accessed=20 * rows * width, transcendentals=0
        ),
        name="finish",
    )(grads, slopes, *backs)
    return (attn_out, grad_queries, grad_keys, grad_values, grad_scale)


def solution(mesh):
    rows = P(("dp", "seq"), None)
    return jax.shard_map(
        functools.partial(on_device, (mesh.shape["dp"], mesh.shape["seq"])),
        mesh=mesh,
        in_specs=(rows, rows, rows, rows, P(), P("dp", None)),
        out_specs=(rows, rows, rows, rows, P()),
        check_vma=False,
    )
```

profile of v0, /device:TPU:0, one launch (start us, length us, event | category | flops | bytes accessed | tf_op | source)
XLA Modules:
  0.0 35.1 jit_solution(13231105430981854075)
XLA Ops:
  0.6 4.9 %collective-permute-start = (bf16[128,512]{1,0:T(8,128)(2,1)}, bf16[128,512]{1,0:T(8,128)(2,1)S(1)}, u32[]{:S(2)}, u32[]{:S(2)}) collective-permute-start(bf16[128,512]{1,0:T(8,128)(2,1)} %key_hbm.1), channel_id=1, source_target_pairs={{0,1},{2,3},{4,5},{6,7},{8,9},{10,11},{12,13},{14,15},{16,17},{18,... | collective-permute-start | bytes 393224 | tf_op jit(solution)/shard_map/ppermute | solution.py:211
  5.5 1.3 %collective-permute-start.1 = (bf16[128,512]{1,0:T(8,128)(2,1)}, bf16[128,512]{1,0:T(8,128)(2,1)S(1)}, u32[]{:S(2)}, u32[]{:S(2)}) collective-permute-start(bf16[128,512]{1,0:T(8,128)(2,1)} %value_hbm.1), channel_id=1, source_target_pairs={{0,1},{2,3},{4,5},{6,7},{8,9},{10,11},{12,13},{14,15},{16,17},{18,... | collective-permute-start | bytes 393224 | tf_op jit(solution)/shard_map/ppermute | solution.py:211
  6.8 2.0 %prep.1 = (bf16[128,4096]{1,0:T(8,128)(2,1)S(1)}, bf16[128,4096]{1,0:T(8,128)(2,1)S(1)}, bf16[128,1024]{1,0:T(8,128)(2,1)S(1)}, f32[128,1024]{1,0:T(8,128)S(1)},...) custom-call(bf16[128,4096]{1,0:T(8,128)(2,1)} %q_hbm.1, bf16[128,4096]{1,0:T(8,128)(2,1)} %g_hbm.1, ...), custom_call_target="tpu_custom_call" | custom-call | flops 6553600 | bytes 1048576 | tf_op jit(solution)/shard_map/prep/pallas_call | solution.py:219
  8.8 0.9 %collective-permute-done.rest_0_ = bf16[128,512]{1,0:T(8,128)(2,1)S(1)} collective-permute-done((bf16[128,512]{1,0:T(8,128)(2,1)}, bf16[128,512]{1,0:T(8,128)(2,1)S(1)}, u32[]{:S(2)}, u32[]{:S(2)}) %collective-permute-start) | collective-permute-done | bytes 131104 | tf_op jit(solution)/shard_map/ppermute | solution.py:211
  9.7 1.7 %collective-permute-done.1.rest_1_ = bf16[128,512]{1,0:T(8,128)(2,1)S(1)} collective-permute-done((bf16[128,512]{1,0:T(8,128)(2,1)}, bf16[128,512]{1,0:T(8,128)(2,1)S(1)}, u32[]{:S(2)}, u32[]{:S(2)}) %collective-permute-start.1) | collective-permute-done | bytes 131104 | tf_op jit(solution)/shard_map/ppermute | solution.py:211
  11.4 5.6 %attend.1 = (bf16[128,4096]{1,0:T(8,128)(2,1)}, bf16[128,4096]{1,0:T(8,128)(2,1)}, f32[128,1024]{1,0:T(8,128)S(1)}, bf16[128,1024]{1,0:T(8,128)(2,1)S(1)}, f32[32,8,128]{2,1,0:T(8,128)S(1)}) custom-call(bf16[128,4096]{1,0:T(8,128)(2,1)S(1)} %get-tuple-element.19.q_ref, bf16[128,4096]{1,0:T(8,128)(2,1)S(1)} %get-tuple-element.20.g_ref, ...), custom_call_target="tpu_custom_call" | custom-call | flops 1610612736 | bytes 4194304 | tf_op jit(solution)/shard_map/attend/pallas_call | solution.py:245
  17.0 1.3 %collective-permute-start.2 = (bf16[128,1024]{1,0:T(8,128)(2,1)S(1)}, bf16[128,1024]{1,0:T(8,128)(2,1)S(1)}, u32[]{:S(2)}, u32[]{:S(2)}) collective-permute-start(bf16[128,1024]{1,0:T(8,128)(2,1)S(1)} %get-tuple-element.29), channel_id=1, source_target_pairs={{1,0},{3,2},{5,4},{7,6},{9,8},{11,10},{13,12},{15,14},{17,16},{19,... | collective-permute-start | bytes 786440 | tf_op jit(solution)/shard_map/ppermute | solution.py:214
  18.3 15.4 %all_to_all.5 = f32[32,8,128]{2,1,0:T(8,128)S(1)} all-to-all(f32[32,8,128]{2,1,0:T(8,128)S(1)} %get-tuple-element.32), channel_id=1, replica_groups=mesh['dp'=16,'seq'=2] {'dp','seq'}, dimensions={0} | all-to-all | bytes 262144 | tf_op jit(solution)/shard_map/all_to_all | solution.py:276
  33.7 0.6 %reduce_sum.9 = f32[8,128]{1,0:T(8,128)} reduce(f32[32,8,128]{2,1,0:T(8,128)S(1)} %all_to_all.5, f32[]{:T(128)} %constant.0.clone.1), dimensions={0}, to_apply=%region_0.0 | reduce | flops 31744 | bytes 135172 | tf_op jit(solution)/shard_map/reduce_sum | solution.py:277
  34.4 0.0 collective-permute-done.2.rest_0_
  34.4 0.8 %finish.1 = (bf16[128,512]{1,0:T(8,128)(2,1)}, bf16[128,512]{1,0:T(8,128)(2,1)}) custom-call(f32[128,1024]{1,0:T(8,128)S(1)} %get-tuple-element.27.grad_ref, f32[128,1024]{1,0:T(8,128)S(1)} %get-tuple-element.28.slope_ref, bf16[128,1024]{1,0:T(8,128)(2,1)S(1)} %collective-permute-done.2.rest_0_), custom_call_target="tpu_custom_call" | custom-call | flops 393216 | bytes 1310720 | tf_op jit(solution)/shard_map/finish/pallas_call | solution.py:279
Async XLA Ops:
  0.6 9.1 %collective-permute-start = (bf16[128,512]{1,0:T(8,128)(2,1)}, bf16[128,512]{1,0:T(8,128)(2,1)S(1)}, u32[]{:S(2)}, u32[]{:S(2)}) collective-permute-start(bf16[128,512]{1,0:T(8,128)(2,1)} %key_hbm.1), channel_id=1, source_target_pairs={{0,1},{2,3},{4,5},{6,7},{8,9},{10,11},{12,13},{14,15},{16,17},{18,... | collective-permute-start | bytes 393224 | tf_op jit(solution)/shard_map/ppermute | solution.py:211
  5.5 5.9 %collective-permute-start.1 = (bf16[128,512]{1,0:T(8,128)(2,1)}, bf16[128,512]{1,0:T(8,128)(2,1)S(1)}, u32[]{:S(2)}, u32[]{:S(2)}) collective-permute-start(bf16[128,512]{1,0:T(8,128)(2,1)} %value_hbm.1), channel_id=1, source_target_pairs={{0,1},{2,3},{4,5},{6,7},{8,9},{10,11},{12,13},{14,15},{16,17},{18,... | collective-permute-start | bytes 393224 | tf_op jit(solution)/shard_map/ppermute | solution.py:211
  17.0 17.3 %collective-permute-start.2 = (bf16[128,1024]{1,0:T(8,128)(2,1)S(1)}, bf16[128,1024]{1,0:T(8,128)(2,1)S(1)}, u32[]{:S(2)}, u32[]{:S(2)}) collective-permute-start(bf16[128,1024]{1,0:T(8,128)(2,1)S(1)} %get-tuple-element.29), channel_id=1, source_target_pairs={{1,0},{3,2},{5,4},{7,6},{9,8},{11,10},{13,12},{15,14},{17,16},{19,... | collective-permute-start | bytes 786440 | tf_op jit(solution)/shard_map/ppermute | solution.py:214
where the time goes:
time: 35.3 us; the launch traced here: 35.1 us
  blocking collectives  15.4 us (44%)
  Pallas kernels  8.38 us (24%)
  starting transfers between devices  7.47 us (21%)
  waiting for transfers between devices  2.55 us (7%)
  between operations  0.68 us (2%)
  other arithmetic  0.63 us (2%)
    all_to_all x1, blocking collectives, on_device(): lax.all_to_all(spread, ('dp', 'seq'), split_axis=0, concat_axis=0, tiled=...  15.4 us
    ppermute x2, starting transfers between devices, shift(): lax.ppermute(array, 'seq', [(r, r + d) for r in range(seq_count - d)])  6.17 us
    pallas_call x1, Pallas kernels, on_device(): pl.pallas_call(functools.partial(attend_kernel, nb), out_shape=(shape(que...  5.64 us
    ppermute x2, waiting for transfers between devices, shift(): lax.ppermute(array, 'seq', [(r, r + d) for r in range(seq_count - d)])  2.55 us
    pallas_call x1, Pallas kernels, on_device(): pl.pallas_call(functools.partial(prep_kernel, nb), out_shape=(shape(queri...  1.99 us
    ppermute x1, starting transfers between devices, unshift(): lax.ppermute(array, 'seq', [(r + d, r) for r in range(seq_count - d)])  1.29 us
    pallas_call x1, Pallas kernels, on_device(): pl.pallas_call(functools.partial(finish_kernel, nb), out_shape=(shape((ro...  0.76 us
  transfers between devices with their start and end apart: 3, of which 2 were waited for; matrix products, arithmetic and copies ran while one was open for 2% of the time, Pallas kernels for 6%

commit v1 on v0

--- a/solution.py
+++ b/solution.py
@@ -85,7 +85,7 @@
 
 def attend_kernel(nb, q_ref, g_ref, quant_ref, dclip_ref, bias_ref, clip_ref, *rest):
     far_k, far_v = rest[:nb], rest[nb:2 * nb]
-    out_hbm, gq_hbm, grad_ref, far_ref, spread_ref, out_ref, gq_ref, scale_ref, sems = rest[2 * nb:]
+    out_hbm, gq_hbm, grad_ref, far_ref, scale_ref, out_ref, gq_ref, sems = rest[2 * nb:]
     kv_heads, hd = clip_ref.shape[1], clip_ref.shape[2]
     rows, group = q_ref.shape[0], q_ref.shape[1] // kv_heads
     heads = group // hd
@@ -173,20 +173,14 @@
         return carry
 
     lax.fori_loop(0, kv_heads, step, 0)
-    part = scale_ref[...]
-
-    def spread(i, carry):
-        spread_ref[i] = part
-        return carry
-
-    lax.fori_loop(0, spread_ref.shape[0], spread, 0)
     for n in range(kv_heads):
         for copy in copies(n):
             copy.wait()
 
 
-def finish_kernel(nb, grad_ref, slope_ref, *rest):
-    backs, (gk_ref, gv_ref) = rest[:nb], rest[nb:]
+def finish_kernel(nb, part_ref, other_ref, grad_ref, slope_ref, *rest):
+    backs, (gk_ref, gv_ref, gs_ref) = rest[:nb], rest[nb:]
+    gs_ref[...] = part_ref[...] + other_ref[...]
     width = gk_ref.shape[1]
     for side, out in ((0, gk_ref), (1, gv_ref)):
         at = slice(side * width, (side + 1) * width)
@@ -196,9 +190,19 @@
         out[...] = (total * slope_ref[:, at]).astype(BF16)
 
 
+def all_sum(part, dp_count, seq_count):
+    count = dp_count * seq_count
+    strides = [seq_count << b for b in range(dp_count.bit_length() - 1)]
+    strides += [1 << b for b in range(seq_count.bit_length() - 1)]
+    for stride in strides:
+        other = lax.ppermute(part, ("dp", "seq"), [(i, i ^ stride) for i in range(count)])
+        if stride == strides[-1]:
+            return part, other
+        part = part + other
+
+
 def on_device(sizes, queries, keys, values, grad_out, quant_scale, doc_lengths):
     dp_count, seq_count = sizes
-    count = dp_count * seq_count
     nb = max(1, seq_count // 2)
     rows, width = keys.shape
     kv_heads, hd = quant_scale.shape[1], quant_scale.shape[2]
@@ -242,21 +246,20 @@
         name="prep",
     )(*[pltpu.with_memory_space_constraint(x, pltpu.HBM) for x in (queries, grad_out, keys, values, quant_scale, doc_lengths)])
 
-    attn_out, grad_queries, grads, far_grads, spread = pl.pallas_call(
+    attn_out, grad_queries, grads, far_grads, scale_part = pl.pallas_call(
         functools.partial(attend_kernel, nb),
         out_shape=(
             shape(queries.shape, BF16),
             shape(queries.shape, BF16),
             shape((rows, 2 * width), F32),
             shape((nb * rows, 2 * width), BF16),
-            shape((count, 2 * kv_heads, hd), F32),
+            shape((2 * kv_heads, hd), F32),
         ),
         in_specs=[vmem] * (6 + 2 * nb),
         out_specs=(hbm, hbm, vmem, vmem, vmem),
         scratch_shapes=[
             pltpu.VMEM(queries.shape, BF16),
             pltpu.VMEM(queries.shape, BF16),
-            pltpu.VMEM((2 * kv_heads, hd), F32),
             pltpu.SemaphoreType.DMA((2, kv_heads)),
         ],
         compiler_params=params,
@@ -273,21 +276,20 @@
     for d in range(1, nb + 1):
         at = order.index(d) * rows
         backs.append(unshift(lax.slice_in_dim(far_grads, at, at + rows, axis=0), d))
-    gathered = lax.all_to_all(spread, ("dp", "seq"), split_axis=0, concat_axis=0, tiled=True)
-    grad_scale = jnp.sum(gathered, axis=0).reshape(quant_scale.shape)
-
-    grad_keys, grad_values = pl.pallas_call(
+    part, other = all_sum(scale_part, dp_count, seq_count)
+
+    grad_keys, grad_values, grad_scale = pl.pallas_call(
         functools.partial(finish_kernel, nb),
-        out_shape=(shape((rows, width), BF16), shape((rows, width), BF16)),
-        in_specs=[vmem] * (2 + nb),
-        out_specs=(vmem, vmem),
+        out_shape=(shape((rows, width), BF16), shape((rows, width), BF16), shape(part.shape, F32)),
+        in_specs=[vmem] * (4 + nb),
+        out_specs=(vmem, vmem, vmem),
         compiler_params=params,
         cost_estimate=pl.CostEstimate(
             flops=6 * rows * width, bytes_accessed=20 * rows * width, transcendentals=0
         ),
         name="finish",
-    )(grads, slopes, *backs)
-    return (attn_out, grad_queries, grad_keys, grad_values, grad_scale)
+    )(part, other, grads, slopes, *backs)
+    return (attn_out, grad_queries, grad_keys, grad_values, grad_scale.reshape(quant_scale.shape))
 
 
 def solution(mesh):

time: 35.3 us -> 36.5 us (1.034)
  blocking collectives: 15.4 us -> 0 us
  waiting for transfers between devices: 2.55 us -> 11.4 us
  starting transfers between devices: 7.47 us -> 15.8 us
  other arithmetic: 0.63 us -> 0.01 us
    all_to_all x1 -> x0, blocking collectives: 15.4 us -> none  [on_device(): lax.all_to_all(spread, ('dp', 'seq'), split_axis=0, concat_axis=0, tiled=...]
    ppermute x0 -> x5, waiting for transfers between devices: none -> 8.8 us  [all_sum(): lax.ppermute(part, ('dp', 'seq'), [(i, i ^ stride) for i in range(count)])]
    ppermute x0 -> x5, starting transfers between devices: none -> 8.38 us  [all_sum(): lax.ppermute(part, ('dp', 'seq'), [(i, i ^ stride) for i in range(count)])]
    reduce_sum x1 -> x0, other arithmetic: 0.63 us -> none  [on_device(): grad_scale = jnp.sum(gathered, axis=0).reshape(quant_scale.shape)]
  transfers between devices with their start and end apart: 3 -> 8, of which waited for: 2 -> 7; matrix products, arithmetic and copies ran while one was open for 2% -> 0% of each run, Pallas kernels for 6% -> 5%
where the time goes in v1:
time: 36.5 us; the launch traced here: 36.3 us
  starting transfers between devices  15.8 us (43%)
  waiting for transfers between devices  11.4 us (31%)
  Pallas kernels  8.41 us (23%)
  between operations  0.69 us (2%)
    ppermute x5, waiting for transfers between devices, all_sum(): lax.ppermute(part, ('dp', 'seq'), [(i, i ^ stride) for i in range(count)])  8.8 us
    ppermute x5, starting transfers between devices, all_sum(): lax.ppermute(part, ('dp', 'seq'), [(i, i ^ stride) for i in range(count)])  8.38 us
    ppermute x2, starting transfers between devices, shift(): lax.ppermute(array, 'seq', [(r, r + d) for r in range(seq_count - d)])  6.17 us
    pallas_call x1, Pallas kernels, on_device(): pl.pallas_call(functools.partial(attend_kernel, nb), out_shape=(shape(que...  5.64 us
    ppermute x2, waiting for transfers between devices, shift(): lax.ppermute(array, 'seq', [(r, r + d) for r in range(seq_count - d)])  2.56 us
    pallas_call x1, Pallas kernels, on_device(): pl.pallas_call(functools.partial(prep_kernel, nb), out_shape=(shape(queri...  1.98 us
    ppermute x1, starting transfers between devices, unshift(): lax.ppermute(array, 'seq', [(r + d, r) for r in range(seq_count - d)])  1.29 us
    pallas_call x1, Pallas kernels, on_device(): pl.pallas_call(functools.partial(finish_kernel, nb), out_shape=(shape((ro...  0.79 us
  transfers between devices with their start and end apart: 8, of which 7 were waited for; matrix products, arithmetic and copies ran while one was open for 0% of the time, Pallas kernels for 5%

profile of v1, /device:TPU:0, one launch (start us, length us, event | category | flops | bytes accessed | tf_op | source)
XLA Modules:
  0.0 36.3 jit_solution(4837104747445233205)
XLA Ops:
  0.6 4.9 %collective-permute-start = (bf16[128,512]{1,0:T(8,128)(2,1)}, bf16[128,512]{1,0:T(8,128)(2,1)S(1)}, u32[]{:S(2)}, u32[]{:S(2)}) collective-permute-start(bf16[128,512]{1,0:T(8,128)(2,1)} %key_hbm.1), channel_id=1, source_target_pairs={{0,1},{2,3},{4,5},{6,7},{8,9},{10,11},{12,13},{14,15},{16,17},{18,... | collective-permute-start | bytes 393224 | tf_op jit(solution)/shard_map/ppermute | solution.py:215
  5.5 1.3 %collective-permute-start.1 = (bf16[128,512]{1,0:T(8,128)(2,1)}, bf16[128,512]{1,0:T(8,128)(2,1)S(1)}, u32[]{:S(2)}, u32[]{:S(2)}) collective-permute-start(bf16[128,512]{1,0:T(8,128)(2,1)} %value_hbm.1), channel_id=1, source_target_pairs={{0,1},{2,3},{4,5},{6,7},{8,9},{10,11},{12,13},{14,15},{16,17},{18,... | collective-permute-start | bytes 393224 | tf_op jit(solution)/shard_map/ppermute | solution.py:215
  6.8 2.0 %prep.1 = (bf16[128,4096]{1,0:T(8,128)(2,1)S(1)}, bf16[128,4096]{1,0:T(8,128)(2,1)S(1)}, bf16[128,1024]{1,0:T(8,128)(2,1)S(1)}, f32[128,1024]{1,0:T(8,128)S(1)},...) custom-call(bf16[128,4096]{1,0:T(8,128)(2,1)} %q_hbm.1, bf16[128,4096]{1,0:T(8,128)(2,1)} %g_hbm.1, ...), custom_call_target="tpu_custom_call" | custom-call | flops 6553600 | bytes 1048576 | tf_op jit(solution)/shard_map/prep/pallas_call | solution.py:223
  8.8 0.9 %collective-permute-done.rest_0_ = bf16[128,512]{1,0:T(8,128)(2,1)S(1)} collective-permute-done((bf16[128,512]{1,0:T(8,128)(2,1)}, bf16[128,512]{1,0:T(8,128)(2,1)S(1)}, u32[]{:S(2)}, u32[]{:S(2)}) %collective-permute-start) | collective-permute-done | bytes 131104 | tf_op jit(solution)/shard_map/ppermute | solution.py:215
  9.7 1.7 %collective-permute-done.1.rest_1_ = bf16[128,512]{1,0:T(8,128)(2,1)S(1)} collective-permute-done((bf16[128,512]{1,0:T(8,128)(2,1)}, bf16[128,512]{1,0:T(8,128)(2,1)S(1)}, u32[]{:S(2)}, u32[]{:S(2)}) %collective-permute-start.1) | collective-permute-done | bytes 131104 | tf_op jit(solution)/shard_map/ppermute | solution.py:215
  11.4 5.6 %attend.1 = (bf16[128,4096]{1,0:T(8,128)(2,1)}, bf16[128,4096]{1,0:T(8,128)(2,1)}, f32[128,1024]{1,0:T(8,128)S(1)}, bf16[128,1024]{1,0:T(8,128)(2,1)S(1)}, f32[8,128]{1,0:T(8,128)S(1)}) custom-call(bf16[128,4096]{1,0:T(8,128)(2,1)S(1)} %get-tuple-element.20.q_ref, bf16[128,4096]{1,0:T(8,128)(2,1)S(1)} %get-tuple-element.21.g_ref, ...), custom_call_target="tpu_custom_call" | custom-call | flops 1610612736 | bytes 4194304 | tf_op jit(solution)/shard_map/attend/pallas_call | solution.py:249
  17.0 1.3 %collective-permute-start.7 = (bf16[128,1024]{1,0:T(8,128)(2,1)S(1)}, bf16[128,1024]{1,0:T(8,128)(2,1)S(1)}, u32[]{:S(2)}, u32[]{:S(2)}) collective-permute-start(bf16[128,1024]{1,0:T(8,128)(2,1)S(1)} %get-tuple-element.31), channel_id=1, source_target_pairs={{1,0},{3,2},{5,4},{7,6},{9,8},{11,10},{13,12},{15,14},{17,16},{19,... | collective-permute-start | bytes 786440 | tf_op jit(solution)/shard_map/ppermute | solution.py:218
  18.3 0.1 collective-permute-start.2
  18.4 1.2 %collective-permute-done.2 = f32[8,128]{1,0:T(8,128)S(1)} collective-permute-done((f32[8,128]{1,0:T(8,128)S(1)}, f32[8,128]{1,0:T(8,128)S(1)}, u32[]{:S(2)}, u32[]{:S(2)}) %collective-permute-start.2) | collective-permute-done | bytes 4128 | tf_op jit(solution)/shard_map/ppermute | solution.py:198
  19.6 1.5 %collective-permute-start.3 = (f32[8,128]{1,0:T(8,128)S(1)}, f32[8,128]{1,0:T(8,128)S(1)}, u32[]{:S(2)}, u32[]{:S(2)}) collective-permute-start(f32[8,128]{1,0:T(8,128)S(1)} %add.12), channel_id=1, source_target_pairs={{0,4},{1,5},{2,6},{3,7},{4,0},{5,1},{6,2},{7,3},{8,12},{9,13},{10,... | collective-permute-start | bytes 12296 | tf_op jit(solution)/shard_map/ppermute | solution.py:198
  21.0 2.1 %collective-permute-done.3 = f32[8,128]{1,0:T(8,128)S(1)} collective-permute-done((f32[8,128]{1,0:T(8,128)S(1)}, f32[8,128]{1,0:T(8,128)S(1)}, u32[]{:S(2)}, u32[]{:S(2)}) %collective-permute-start.3) | collective-permute-done | bytes 4128 | tf_op jit(solution)/shard_map/ppermute | solution.py:198
  23.2 1.6 %collective-permute-start.4 = (f32[8,128]{1,0:T(8,128)S(1)}, f32[8,128]{1,0:T(8,128)S(1)}, u32[]{:S(2)}, u32[]{:S(2)}) collective-permute-start(f32[8,128]{1,0:T(8,128)S(1)} %add.13), channel_id=1, source_target_pairs={{0,8},{1,9},{2,10},{3,11},{4,12},{5,13},{6,14},{7,15},{8,0},{9,1},... | collective-permute-start | bytes 12296 | tf_op jit(solution)/shard_map/ppermute | solution.py:198
  24.7 2.0 %collective-permute-done.4 = f32[8,128]{1,0:T(8,128)S(1)} collective-permute-done((f32[8,128]{1,0:T(8,128)S(1)}, f32[8,128]{1,0:T(8,128)S(1)}, u32[]{:S(2)}, u32[]{:S(2)}) %collective-permute-start.4) | collective-permute-done | bytes 4128 | tf_op jit(solution)/shard_map/ppermute | solution.py:198
  26.8 2.6 %collective-permute-start.5 = (f32[8,128]{1,0:T(8,128)S(1)}, f32[8,128]{1,0:T(8,128)S(1)}, u32[]{:S(2)}, u32[]{:S(2)}) collective-permute-start(f32[8,128]{1,0:T(8,128)S(1)} %add.14), channel_id=1, source_target_pairs={{0,16},{1,17},{2,18},{3,19},{4,20},{5,21},{6,22},{7,23},{8,24},{9,... | collective-permute-start | bytes 12296 | tf_op jit(solution)/shard_map/ppermute | solution.py:198
  29.4 1.9 %collective-permute-done.5 = f32[8,128]{1,0:T(8,128)S(1)} collective-permute-done((f32[8,128]{1,0:T(8,128)S(1)}, f32[8,128]{1,0:T(8,128)S(1)}, u32[]{:S(2)}, u32[]{:S(2)}) %collective-permute-start.5) | collective-permute-done | bytes 4128 | tf_op jit(solution)/shard_map/ppermute | solution.py:198
  31.3 2.7 %collective-permute-start.6 = (f32[8,128]{1,0:T(8,128)S(1)}, f32[8,128]{1,0:T(8,128)S(1)}, u32[]{:S(2)}, u32[]{:S(2)}) collective-permute-start(f32[8,128]{1,0:T(8,128)S(1)} %add.15.part_ref), channel_id=1, source_target_pairs={{0,1},{1,0},{2,3},{3,2},{4,5},{5,4},{6,7},{7,6},{8,9},{9,8},{10,11... | collective-permute-start | bytes 12296 | tf_op jit(solution)/shard_map/ppermute | solution.py:198
  33.9 1.6 %collective-permute-done.6.other_ref = f32[8,128]{1,0:T(8,128)S(1)} collective-permute-done((f32[8,128]{1,0:T(8,128)S(1)}, f32[8,128]{1,0:T(8,128)S(1)}, u32[]{:S(2)}, u32[]{:S(2)}) %collective-permute-start.6) | collective-permute-done | bytes 4128 | tf_op jit(solution)/shard_map/ppermute | solution.py:198
  35.5 0.0 collective-permute-done.7.rest_0_
  35.5 0.8 %finish.1 = (bf16[128,512]{1,0:T(8,128)(2,1)}, bf16[128,512]{1,0:T(8,128)(2,1)}, f32[8,128]{1,0:T(8,128)}) custom-call(f32[8,128]{1,0:T(8,128)S(1)} %add.15.part_ref, f32[8,128]{1,0:T(8,128)S(1)} %collective-permute-done.6.other_ref, f32[128,1024]{1,0:T(8,128)S(1)} %get-tuple-element.29.grad_ref, f32[128,1024]{1,0:T(8,128)S(1)} %get-tuple-element.30.slope_ref, ...), custom_call_target="tpu_custom_call" | custom-call | flops 393216 | bytes 1310720 | tf_op jit(solution)/shard_map/finish/pallas_call | solution.py:281
  (4 shorter events, 0.0 us)
Async XLA Ops:
  0.6 9.1 %collective-permute-start = (bf16[128,512]{1,0:T(8,128)(2,1)}, bf16[128,512]{1,0:T(8,128)(2,1)S(1)}, u32[]{:S(2)}, u32[]{:S(2)}) collective-permute-start(bf16[128,512]{1,0:T(8,128)(2,1)} %key_hbm.1), channel_id=1, source_target_pairs={{0,1},{2,3},{4,5},{6,7},{8,9},{10,11},{12,13},{14,15},{16,17},{18,... | collective-permute-start | bytes 393224 | tf_op jit(solution)/shard_map/ppermute | solution.py:215
  5.5 5.9 %collective-permute-start.1 = (bf16[128,512]{1,0:T(8,128)(2,1)}, bf16[128,512]{1,0:T(8,128)(2,1)S(1)}, u32[]{:S(2)}, u32[]{:S(2)}) collective-permute-start(bf16[128,512]{1,0:T(8,128)(2,1)} %value_hbm.1), channel_id=1, source_target_pairs={{0,1},{2,3},{4,5},{6,7},{8,9},{10,11},{12,13},{14,15},{16,17},{18,... | collective-permute-start | bytes 393224 | tf_op jit(solution)/shard_map/ppermute | solution.py:215
  17.0 18.5 %collective-permute-start.7 = (bf16[128,1024]{1,0:T(8,128)(2,1)S(1)}, bf16[128,1024]{1,0:T(8,128)(2,1)S(1)}, u32[]{:S(2)}, u32[]{:S(2)}) collective-permute-start(bf16[128,1024]{1,0:T(8,128)(2,1)S(1)} %get-tuple-element.31), channel_id=1, source_target_pairs={{1,0},{3,2},{5,4},{7,6},{9,8},{11,10},{13,12},{15,14},{17,16},{19,... | collective-permute-start | bytes 786440 | tf_op jit(solution)/shard_map/ppermute | solution.py:218
  18.3 1.2 %collective-permute-start.2 = (f32[8,128]{1,0:T(8,128)S(1)}, f32[8,128]{1,0:T(8,128)S(1)}, u32[]{:S(2)}, u32[]{:S(2)}) collective-permute-start(f32[8,128]{1,0:T(8,128)S(1)} %get-tuple-element.28), channel_id=1, source_target_pairs={{0,2},{1,3},{2,0},{3,1},{4,6},{5,7},{6,4},{7,5},{8,10},{9,11},{10,... | collective-permute-start | bytes 12296 | tf_op jit(solution)/shard_map/ppermute | solution.py:198
  19.6 3.6 %collective-permute-start.3 = (f32[8,128]{1,0:T(8,128)S(1)}, f32[8,128]{1,0:T(8,128)S(1)}, u32[]{:S(2)}, u32[]{:S(2)}) collective-permute-start(f32[8,128]{1,0:T(8,128)S(1)} %add.12), channel_id=1, source_target_pairs={{0,4},{1,5},{2,6},{3,7},{4,0},{5,1},{6,2},{7,3},{8,12},{9,13},{10,... | collective-permute-start | bytes 12296 | tf_op jit(solution)/shard_map/ppermute | solution.py:198
  23.2 3.6 %collective-permute-start.4 = (f32[8,128]{1,0:T(8,128)S(1)}, f32[8,128]{1,0:T(8,128)S(1)}, u32[]{:S(2)}, u32[]{:S(2)}) collective-permute-start(f32[8,128]{1,0:T(8,128)S(1)} %add.13), channel_id=1, source_target_pairs={{0,8},{1,9},{2,10},{3,11},{4,12},{5,13},{6,14},{7,15},{8,0},{9,1},... | collective-permute-start | bytes 12296 | tf_op jit(solution)/shard_map/ppermute | solution.py:198
  26.8 4.5 %collective-permute-start.5 = (f32[8,128]{1,0:T(8,128)S(1)}, f32[8,128]{1,0:T(8,128)S(1)}, u32[]{:S(2)}, u32[]{:S(2)}) collective-permute-start(f32[8,128]{1,0:T(8,128)S(1)} %add.14), channel_id=1, source_target_pairs={{0,16},{1,17},{2,18},{3,19},{4,20},{5,21},{6,22},{7,23},{8,24},{9,... | collective-permute-start | bytes 12296 | tf_op jit(solution)/shard_map/ppermute | solution.py:198
  31.3 4.2 %collective-permute-start.6 = (f32[8,128]{1,0:T(8,128)S(1)}, f32[8,128]{1,0:T(8,128)S(1)}, u32[]{:S(2)}, u32[]{:S(2)}) collective-permute-start(f32[8,128]{1,0:T(8,128)S(1)} %add.15.part_ref), channel_id=1, source_target_pairs={{0,1},{1,0},{2,3},{3,2},{4,5},{5,4},{6,7},{7,6},{8,9},{9,8},{10,11... | collective-permute-start | bytes 12296 | tf_op jit(solution)/shard_map/ppermute | solution.py:198

commit v2 on v1

--- a/solution.py
+++ b/solution.py
@@ -191,14 +191,29 @@
 
 
 def all_sum(part, dp_count, seq_count):
+    axes = ("dp", "seq")
     count = dp_count * seq_count
-    strides = [seq_count << b for b in range(dp_count.bit_length() - 1)]
-    strides += [1 << b for b in range(seq_count.bit_length() - 1)]
-    for stride in strides:
-        other = lax.ppermute(part, ("dp", "seq"), [(i, i ^ stride) for i in range(count)])
-        if stride == strides[-1]:
-            return part, other
-        part = part + other
+    core = seq_count
+    bits = [1 << b for b in range(count.bit_length() - 1) if (1 << b) != core]
+    fields = [bits[j:j + 2] for j in range(0, len(bits), 2)]
+    part = part + lax.ppermute(part, axes, [(i, i ^ core) for i in range(count)])
+    active = [i for i in range(count) if i & core]
+    levels = []
+    for field in fields:
+        steps = [sum(c) for c in ([field[0]], field[1:], field) if c][:2 ** len(field) - 1]
+        mask = sum(field)
+        root = 0 if field[0] < core else field[0]
+        leaves = [(k, [i for i in active if (i ^ k) & mask == root]) for k in steps]
+        terms = [part] + [lax.ppermute(part, axes, [(i, i ^ k) for i in group]) for k, group in leaves]
+        part = functools.reduce(jnp.add, terms)
+        levels.append(leaves)
+        active = [i for i in active if i & mask == root]
+    total = jnp.where(lax.axis_index(axes) == active[0], part, jnp.zeros_like(part))
+    for leaves in reversed(levels):
+        terms = [total] + [lax.ppermute(total, axes, [(i ^ k, i) for i in group]) for k, group in leaves]
+        total = functools.reduce(jnp.add, terms)
+    other = lax.ppermute(total, axes, [(i, i ^ core) for i in range(count) if i & core])
+    return total, other
 
 
 def on_device(sizes, queries, keys, values, grad_out, quant_scale, doc_lengths):
@@ -212,10 +227,10 @@
     shape = jax.ShapeDtypeStruct
 
     def shift(array, d):
-        return lax.ppermute(array, "seq", [(r, r + d) for r in range(seq_count - d)])
+        return lax.ppermute(array, "seq", [(r, (r + d) % seq_count) for r in range(seq_count)])
 
     def unshift(array, d):
-        return lax.ppermute(array, "seq", [(r + d, r) for r in range(seq_count - d)])
+        return lax.ppermute(array, "seq", [((r + d) % seq_count, r) for r in range(seq_count)])
 
     far_k = [shift(keys, d) for d in range(1, nb + 1)]
     far_v = [shift(values, d) for d in range(1, nb + 1)]

time: 36.5 us -> 46 us (1.26)
  waiting for transfers between devices: 11.4 us -> 22.2 us
  starting transfers between devices: 15.8 us -> 14.2 us
    ppermute x8 -> x17, waiting for transfers between devices: 11.4 us -> 22.2 us  [the longest x1 16.6 us: all_sum(): lax.ppermute(total, axes, [(i, i ^ core) for i in range(count) if i & core])]
    ppermute x8 -> x17, starting transfers between devices: 15.8 us -> 14.2 us  [the longest x6 3.97 us: all_sum(): lax.ppermute(total, axes, [(i ^ k, i) for i in group])]
  transfers between devices with their start and end apart: 8 -> 17, of which waited for: 7 -> 4; matrix products, arithmetic and copies ran while one was open for 0% -> 0% of each run, Pallas kernels for 5% -> 4%
where the time goes in v2:
time: 46 us; the launch traced here: 45.7 us
  waiting for transfers between devices  22.2 us (48%)
  starting transfers between devices  14.2 us (31%)
  Pallas kernels  8.39 us (18%)
  between operations  0.87 us (2%)
    ppermute x1, waiting for transfers between devices, all_sum(): lax.ppermute(total, axes, [(i, i ^ core) for i in range(count) if i & core])  16.6 us
    pallas_call x1, Pallas kernels, on_device(): pl.pallas_call(functools.partial(attend_kernel, nb), out_shape=(shape(que...  5.64 us
    ppermute x2, waiting for transfers between devices, shift(): lax.ppermute(array, 'seq', [(r, (r + d) % seq_count) for r in range(seq_c...  4.44 us
    ppermute x6, starting transfers between devices, all_sum(): lax.ppermute(total, axes, [(i ^ k, i) for i in group])  3.97 us
    ppermute x6, starting transfers between devices, all_sum(): lax.ppermute(part, axes, [(i, i ^ k) for i in group])  3.96 us
    ppermute x2, starting transfers between devices, shift(): lax.ppermute(array, 'seq', [(r, (r + d) % seq_count) for r in range(seq_c...  3.11 us
    pallas_call x1, Pallas kernels, on_device(): pl.pallas_call(functools.partial(prep_kernel, nb), out_shape=(shape(queri...  1.99 us
    ppermute x1, starting transfers between devices, unshift(): lax.ppermute(array, 'seq', [((r + d) % seq_count, r) for r in range(seq_c...  1.81 us
  transfers between devices with their start and end apart: 17, of which 4 were waited for; matrix products, arithmetic and copies ran while one was open for 0% of the time, Pallas kernels for 4%

profile of v2, /device:TPU:0, one launch (start us, length us, event | category | flops | bytes accessed | tf_op | source)
XLA Modules:
  0.0 45.7 jit_solution(60848853656833031)
XLA Ops:
  0.6 3.0 %collective-permute-start = (bf16[128,512]{1,0:T(8,128)(2,1)}, bf16[128,512]{1,0:T(8,128)(2,1)S(1)}, u32[]{:S(2)}, u32[]{:S(2)}) collective-permute-start(bf16[128,512]{1,0:T(8,128)(2,1)} %key_hbm.1), channel_id=1, source_target_pairs={{0,1},{1,0},{2,3},{3,2},{4,5},{5,4},{6,7},{7,6},{8,9},{9,8},{10,11... | collective-permute-start | bytes 393224 | tf_op jit(solution)/shard_map/ppermute | solution.py:230
  3.7 0.1 collective-permute-start.1
  3.7 2.0 %prep.1 = (bf16[128,4096]{1,0:T(8,128)(2,1)S(1)}, bf16[128,4096]{1,0:T(8,128)(2,1)S(1)}, bf16[128,1024]{1,0:T(8,128)(2,1)S(1)}, f32[128,1024]{1,0:T(8,128)S(1)},...) custom-call(bf16[128,4096]{1,0:T(8,128)(2,1)} %q_hbm.1, bf16[128,4096]{1,0:T(8,128)(2,1)} %g_hbm.1, ...), custom_call_target="tpu_custom_call" | custom-call | flops 6553600 | bytes 1048576 | tf_op jit(solution)/shard_map/prep/pallas_call | solution.py:238
  5.7 2.5 %collective-permute-done.rest_0_ = bf16[128,512]{1,0:T(8,128)(2,1)S(1)} collective-permute-done((bf16[128,512]{1,0:T(8,128)(2,1)}, bf16[128,512]{1,0:T(8,128)(2,1)S(1)}, u32[]{:S(2)}, u32[]{:S(2)}) %collective-permute-start) | collective-permute-done | bytes 131104 | tf_op jit(solution)/shard_map/ppermute | solution.py:230
  8.2 2.0 %collective-permute-done.1.rest_1_ = bf16[128,512]{1,0:T(8,128)(2,1)S(1)} collective-permute-done((bf16[128,512]{1,0:T(8,128)(2,1)}, bf16[128,512]{1,0:T(8,128)(2,1)S(1)}, u32[]{:S(2)}, u32[]{:S(2)}) %collective-permute-start.1) | collective-permute-done | bytes 131104 | tf_op jit(solution)/shard_map/ppermute | solution.py:230
  10.2 5.6 %attend.1 = (bf16[128,4096]{1,0:T(8,128)(2,1)}, bf16[128,4096]{1,0:T(8,128)(2,1)}, f32[128,1024]{1,0:T(8,128)S(1)}, bf16[128,1024]{1,0:T(8,128)(2,1)S(1)}, f32[8,128]{1,0:T(8,128)S(1)}) custom-call(bf16[128,4096]{1,0:T(8,128)(2,1)S(1)} %get-tuple-element.20.q_ref, bf16[128,4096]{1,0:T(8,128)(2,1)S(1)} %get-tuple-element.21.g_ref, ...), custom_call_target="tpu_custom_call" | custom-call | flops 1610612736 | bytes 4194304 | tf_op jit(solution)/shard_map/attend/pallas_call | solution.py:264
  15.8 0.1 collective-permute-start.2
  15.9 1.2 %collective-permute-done.2 = f32[8,128]{1,0:T(8,128)S(1)} collective-permute-done((f32[8,128]{1,0:T(8,128)S(1)}, f32[8,128]{1,0:T(8,128)S(1)}, u32[]{:S(2)}, u32[]{:S(2)}) %collective-permute-start.2) | collective-permute-done | bytes 4128 | tf_op jit(solution)/shard_map/ppermute | solution.py:199
  17.1 0.7 %collective-permute-start.3 = (f32[8,128]{1,0:T(8,128)S(1)}, f32[8,128]{1,0:T(8,128)S(1)}, u32[]{:S(2)}, u32[]{:S(2)}) collective-permute-start(f32[8,128]{1,0:T(8,128)S(1)} %add.43), channel_id=1, source_target_pairs={{3,2},{11,10},{19,18},{27,26}} | collective-permute-start | bytes 12296 | tf_op jit(solution)/shard_map/ppermute | solution.py:207
  17.7 0.7 %collective-permute-start.4 = (f32[8,128]{1,0:T(8,128)S(1)}, f32[8,128]{1,0:T(8,128)S(1)}, u32[]{:S(2)}, u32[]{:S(2)}) collective-permute-start(f32[8,128]{1,0:T(8,128)S(1)} %add.43), channel_id=1, source_target_pairs={{6,2},{14,10},{22,18},{30,26}} | collective-permute-start | bytes 12296 | tf_op jit(solution)/shard_map/ppermute | solution.py:207
  18.4 0.7 %collective-permute-start.5 = (f32[8,128]{1,0:T(8,128)S(1)}, f32[8,128]{1,0:T(8,128)S(1)}, u32[]{:S(2)}, u32[]{:S(2)}) collective-permute-start(f32[8,128]{1,0:T(8,128)S(1)} %add.43), channel_id=1, source_target_pairs={{7,2},{15,10},{23,18},{31,26}} | collective-permute-start | bytes 12296 | tf_op jit(solution)/shard_map/ppermute | solution.py:207
  19.1 0.7 %collective-permute-start.6 = (f32[8,128]{1,0:T(8,128)S(1)}, f32[8,128]{1,0:T(8,128)S(1)}, u32[]{:S(2)}, u32[]{:S(2)}) collective-permute-start(f32[8,128]{1,0:T(8,128)S(1)} %add_add_fusion.2), channel_id=1, source_target_pairs={{2,10}} | collective-permute-start | bytes 12296 | tf_op jit(solution)/shard_map/ppermute | solution.py:207
  19.8 0.7 %collective-permute-start.7 = (f32[8,128]{1,0:T(8,128)S(1)}, f32[8,128]{1,0:T(8,128)S(1)}, u32[]{:S(2)}, u32[]{:S(2)}) collective-permute-start(f32[8,128]{1,0:T(8,128)S(1)} %add_add_fusion.2), channel_id=1, source_target_pairs={{26,10}} | collective-permute-start | bytes 12296 | tf_op jit(solution)/shard_map/ppermute | solution.py:207
  20.4 0.7 %collective-permute-start.8 = (f32[8,128]{1,0:T(8,128)S(1)}, f32[8,128]{1,0:T(8,128)S(1)}, u32[]{:S(2)}, u32[]{:S(2)}) collective-permute-start(f32[8,128]{1,0:T(8,128)S(1)} %add_add_fusion.2), channel_id=1, source_target_pairs={{18,10}} | collective-permute-start | bytes 12296 | tf_op jit(solution)/shard_map/ppermute | solution.py:207
  21.2 0.7 %collective-permute-start.10 = (f32[8,128]{1,0:T(8,128)S(1)}, f32[8,128]{1,0:T(8,128)S(1)}, u32[]{:S(2)}, u32[]{:S(2)}) collective-permute-start(f32[8,128]{1,0:T(8,128)S(1)} %add_select_fusion), channel_id=1, source_target_pairs={{10,26}} | collective-permute-start | bytes 12296 | tf_op jit(solution)/shard_map/ppermute | solution.py:213
  21.8 0.7 %collective-permute-start.11 = (f32[8,128]{1,0:T(8,128)S(1)}, f32[8,128]{1,0:T(8,128)S(1)}, u32[]{:S(2)}, u32[]{:S(2)}) collective-permute-start(f32[8,128]{1,0:T(8,128)S(1)} %add_select_fusion), channel_id=1, source_target_pairs={{10,18}} | collective-permute-start | bytes 12296 | tf_op jit(solution)/shard_map/ppermute | solution.py:213
  22.5 0.7 %collective-permute-start.9 = (f32[8,128]{1,0:T(8,128)S(1)}, f32[8,128]{1,0:T(8,128)S(1)}, u32[]{:S(2)}, u32[]{:S(2)}) collective-permute-start(f32[8,128]{1,0:T(8,128)S(1)} %add_select_fusion), channel_id=1, source_target_pairs={{10,2}} | collective-permute-start | bytes 12296 | tf_op jit(solution)/shard_map/ppermute | solution.py:213
  23.2 1.8 %collective-permute-start.16 = (bf16[128,1024]{1,0:T(8,128)(2,1)S(1)}, bf16[128,1024]{1,0:T(8,128)(2,1)S(1)}, u32[]{:S(2)}, u32[]{:S(2)}) collective-permute-start(bf16[128,1024]{1,0:T(8,128)(2,1)S(1)} %get-tuple-element.31), channel_id=1, source_target_pairs={{1,0},{0,1},{3,2},{2,3},{5,4},{4,5},{7,6},{6,7},{9,8},{8,9},{11,10... | collective-permute-start | bytes 786440 | tf_op jit(solution)/shard_map/ppermute | solution.py:233
  25.0 0.7 %collective-permute-start.12 = (f32[8,128]{1,0:T(8,128)S(1)}, f32[8,128]{1,0:T(8,128)S(1)}, u32[]{:S(2)}, u32[]{:S(2)}) collective-permute-start(f32[8,128]{1,0:T(8,128)S(1)} %add_add_fusion.1), channel_id=1, source_target_pairs={{2,3},{10,11},{18,19},{26,27}} | collective-permute-start | bytes 12296 | tf_op jit(solution)/shard_map/ppermute | solution.py:213
  25.7 0.7 %collective-permute-start.13 = (f32[8,128]{1,0:T(8,128)S(1)}, f32[8,128]{1,0:T(8,128)S(1)}, u32[]{:S(2)}, u32[]{:S(2)}) collective-permute-start(f32[8,128]{1,0:T(8,128)S(1)} %add_add_fusion.1), channel_id=1, source_target_pairs={{2,6},{10,14},{18,22},{26,30}} | collective-permute-start | bytes 12296 | tf_op jit(solution)/shard_map/ppermute | solution.py:213
  26.4 0.7 %collective-permute-start.14 = (f32[8,128]{1,0:T(8,128)S(1)}, f32[8,128]{1,0:T(8,128)S(1)}, u32[]{:S(2)}, u32[]{:S(2)}) collective-permute-start(f32[8,128]{1,0:T(8,128)S(1)} %add_add_fusion.1), channel_id=1, source_target_pairs={{2,7},{10,15},{18,23},{26,31}} | collective-permute-start | bytes 12296 | tf_op jit(solution)/shard_map/ppermute | solution.py:213
  27.1 1.3 %collective-permute-start.15 = (f32[8,128]{1,0:T(8,128)S(1)}, f32[8,128]{1,0:T(8,128)S(1)}, u32[]{:S(2)}, u32[]{:S(2)}) collective-permute-start(f32[8,128]{1,0:T(8,128)S(1)} %add_add_fusion.part_ref), channel_id=1, source_target_pairs={{2,0},{3,1},{6,4},{7,5},{10,8},{11,9},{14,12},{15,13},{18,16},{19,... | collective-permute-start | bytes 12296 | tf_op jit(solution)/shard_map/ppermute | solution.py:215
  28.4 16.6 %collective-permute-done.15.other_ref = f32[8,128]{1,0:T(8,128)S(1)} collective-permute-done((f32[8,128]{1,0:T(8,128)S(1)}, f32[8,128]{1,0:T(8,128)S(1)}, u32[]{:S(2)}, u32[]{:S(2)}) %collective-permute-start.15) | collective-permute-done | bytes 4128 | tf_op jit(solution)/shard_map/ppermute | solution.py:215
  45.0 0.8 %finish.1 = (bf16[128,512]{1,0:T(8,128)(2,1)}, bf16[128,512]{1,0:T(8,128)(2,1)}, f32[8,128]{1,0:T(8,128)}) custom-call(f32[8,128]{1,0:T(8,128)S(1)} %add_add_fusion.part_ref, f32[8,128]{1,0:T(8,128)S(1)} %collective-permute-done.15.other_ref, f32[128,1024]{1,0:T(8,128)S(1)} %get-tuple-element.29.grad_ref, f32[128,1024]{1,0:T(8,128)S(1)} %get-tuple-element.30.slope_ref, ...), custom_call_target="tpu_custom_call" | custom-call | flops 393216 | bytes 1310720 | tf_op jit(solution)/shard_map/finish/pallas_call | solution.py:296
  (18 shorter events, 0.1 us)
Async XLA Ops:
  0.6 7.6 %collective-permute-start = (bf16[128,512]{1,0:T(8,128)(2,1)}, bf16[128,512]{1,0:T(8,128)(2,1)S(1)}, u32[]{:S(2)}, u32[]{:S(2)}) collective-permute-start(bf16[128,512]{1,0:T(8,128)(2,1)} %key_hbm.1), channel_id=1, source_target_pairs={{0,1},{1,0},{2,3},{3,2},{4,5},{5,4},{6,7},{7,6},{8,9},{9,8},{10,11... | collective-permute-start | bytes 393224 | tf_op jit(solution)/shard_map/ppermute | solution.py:230
  3.7 6.5 %collective-permute-start.1 = (bf16[128,512]{1,0:T(8,128)(2,1)}, bf16[128,512]{1,0:T(8,128)(2,1)S(1)}, u32[]{:S(2)}, u32[]{:S(2)}) collective-permute-start(bf16[128,512]{1,0:T(8,128)(2,1)} %value_hbm.1), channel_id=1, source_target_pairs={{0,1},{1,0},{2,3},{3,2},{4,5},{5,4},{6,7},{7,6},{8,9},{9,8},{10,11... | collective-permute-start | bytes 393224 | tf_op jit(solution)/shard_map/ppermute | solution.py:230
  15.8 1.2 %collective-permute-start.2 = (f32[8,128]{1,0:T(8,128)S(1)}, f32[8,128]{1,0:T(8,128)S(1)}, u32[]{:S(2)}, u32[]{:S(2)}) collective-permute-start(f32[8,128]{1,0:T(8,128)S(1)} %get-tuple-element.28), channel_id=1, source_target_pairs={{0,2},{1,3},{2,0},{3,1},{4,6},{5,7},{6,4},{7,5},{8,10},{9,11},{10,... | collective-permute-start | bytes 12296 | tf_op jit(solution)/shard_map/ppermute | solution.py:199
  17.1 2.0 %collective-permute-start.3 = (f32[8,128]{1,0:T(8,128)S(1)}, f32[8,128]{1,0:T(8,128)S(1)}, u32[]{:S(2)}, u32[]{:S(2)}) collective-permute-start(f32[8,128]{1,0:T(8,128)S(1)} %add.43), channel_id=1, source_target_pairs={{3,2},{11,10},{19,18},{27,26}} | collective-permute-start | bytes 12296 | tf_op jit(solution)/shard_map/ppermute | solution.py:207
  17.7 1.4 %collective-permute-start.4 = (f32[8,128]{1,0:T(8,128)S(1)}, f32[8,128]{1,0:T(8,128)S(1)}, u32[]{:S(2)}, u32[]{:S(2)}) collective-permute-start(f32[8,128]{1,0:T(8,128)S(1)} %add.43), channel_id=1, source_target_pairs={{6,2},{14,10},{22,18},{30,26}} | collective-permute-start | bytes 12296 | tf_op jit(solution)/shard_map/ppermute | solution.py:207
  18.4 0.7 %collective-permute-start.5 = (f32[8,128]{1,0:T(8,128)S(1)}, f32[8,128]{1,0:T(8,128)S(1)}, u32[]{:S(2)}, u32[]{:S(2)}) collective-permute-start(f32[8,128]{1,0:T(8,128)S(1)} %add.43), channel_id=1, source_target_pairs={{7,2},{15,10},{23,18},{31,26}} | collective-permute-start | bytes 12296 | tf_op jit(solution)/shard_map/ppermute | solution.py:207
  19.1 2.0 %collective-permute-start.6 = (f32[8,128]{1,0:T(8,128)S(1)}, f32[8,128]{1,0:T(8,128)S(1)}, u32[]{:S(2)}, u32[]{:S(2)}) collective-permute-start(f32[8,128]{1,0:T(8,128)S(1)} %add_add_fusion.2), channel_id=1, source_target_pairs={{2,10}} | collective-permute-start | bytes 12296 | tf_op jit(solution)/shard_map/ppermute | solution.py:207
  19.8 1.4 %collective-permute-start.7 = (f32[8,128]{1,0:T(8,128)S(1)}, f32[8,128]{1,0:T(8,128)S(1)}, u32[]{:S(2)}, u32[]{:S(2)}) collective-permute-start(f32[8,128]{1,0:T(8,128)S(1)} %add_add_fusion.2), channel_id=1, source_target_pairs={{26,10}} | collective-permute-start | bytes 12296 | tf_op jit(solution)/shard_map/ppermute | solution.py:207
  20.4 0.7 %collective-permute-start.8 = (f32[8,128]{1,0:T(8,128)S(1)}, f32[8,128]{1,0:T(8,128)S(1)}, u32[]{:S(2)}, u32[]{:S(2)}) collective-permute-start(f32[8,128]{1,0:T(8,128)S(1)} %add_add_fusion.2), channel_id=1, source_target_pairs={{18,10}} | collective-permute-start | bytes 12296 | tf_op jit(solution)/shard_map/ppermute | solution.py:207
  21.2 3.8 %collective-permute-start.10 = (f32[8,128]{1,0:T(8,128)S(1)}, f32[8,128]{1,0:T(8,128)S(1)}, u32[]{:S(2)}, u32[]{:S(2)}) collective-permute-start(f32[8,128]{1,0:T(8,128)S(1)} %add_select_fusion), channel_id=1, source_target_pairs={{10,26}} | collective-permute-start | bytes 12296 | tf_op jit(solution)/shard_map/ppermute | solution.py:213
  21.8 3.2 %collective-permute-start.11 = (f32[8,128]{1,0:T(8,128)S(1)}, f32[8,128]{1,0:T(8,128)S(1)}, u32[]{:S(2)}, u32[]{:S(2)}) collective-permute-start(f32[8,128]{1,0:T(8,128)S(1)} %add_select_fusion), channel_id=1, source_target_pairs={{10,18}} | collective-permute-start | bytes 12296 | tf_op jit(solution)/shard_map/ppermute | solution.py:213
  22.5 2.5 %collective-permute-start.9 = (f32[8,128]{1,0:T(8,128)S(1)}, f32[8,128]{1,0:T(8,128)S(1)}, u32[]{:S(2)}, u32[]{:S(2)}) collective-permute-start(f32[8,128]{1,0:T(8,128)S(1)} %add_select_fusion), channel_id=1, source_target_pairs={{10,2}} | collective-permute-start | bytes 12296 | tf_op jit(solution)/shard_map/ppermute | solution.py:213
  23.2 21.8 %collective-permute-start.16 = (bf16[128,1024]{1,0:T(8,128)(2,1)S(1)}, bf16[128,1024]{1,0:T(8,128)(2,1)S(1)}, u32[]{:S(2)}, u32[]{:S(2)}) collective-permute-start(bf16[128,1024]{1,0:T(8,128)(2,1)S(1)} %get-tuple-element.31), channel_id=1, source_target_pairs={{1,0},{0,1},{3,2},{2,3},{5,4},{4,5},{7,6},{6,7},{9,8},{8,9},{11,10... | collective-permute-start | bytes 786440 | tf_op jit(solution)/shard_map/ppermute | solution.py:233
  25.0 2.0 %collective-permute-start.12 = (f32[8,128]{1,0:T(8,128)S(1)}, f32[8,128]{1,0:T(8,128)S(1)}, u32[]{:S(2)}, u32[]{:S(2)}) collective-permute-start(f32[8,128]{1,0:T(8,128)S(1)} %add_add_fusion.1), channel_id=1, source_target_pairs={{2,3},{10,11},{18,19},{26,27}} | collective-permute-start | bytes 12296 | tf_op jit(solution)/shard_map/ppermute | solution.py:213
  25.7 1.4 %collective-permute-start.13 = (f32[8,128]{1,0:T(8,128)S(1)}, f32[8,128]{1,0:T(8,128)S(1)}, u32[]{:S(2)}, u32[]{:S(2)}) collective-permute-start(f32[8,128]{1,0:T(8,128)S(1)} %add_add_fusion.1), channel_id=1, source_target_pairs={{2,6},{10,14},{18,22},{26,30}} | collective-permute-start | bytes 12296 | tf_op jit(solution)/shard_map/ppermute | solution.py:213
  26.4 0.7 %collective-permute-start.14 = (f32[8,128]{1,0:T(8,128)S(1)}, f32[8,128]{1,0:T(8,128)S(1)}, u32[]{:S(2)}, u32[]{:S(2)}) collective-permute-start(f32[8,128]{1,0:T(8,128)S(1)} %add_add_fusion.1), channel_id=1, source_target_pairs={{2,7},{10,15},{18,23},{26,31}} | collective-permute-start | bytes 12296 | tf_op jit(solution)/shard_map/ppermute | solution.py:213
  27.1 17.9 %collective-permute-start.15 = (f32[8,128]{1,0:T(8,128)S(1)}, f32[8,128]{1,0:T(8,128)S(1)}, u32[]{:S(2)}, u32[]{:S(2)}) collective-permute-start(f32[8,128]{1,0:T(8,128)S(1)} %add_add_fusion.part_ref), channel_id=1, source_target_pairs={{2,0},{3,1},{6,4},{7,5},{10,8},{11,9},{14,12},{15,13},{18,16},{19,... | collective-permute-start | bytes 12296 | tf_op jit(solution)/shard_map/ppermute | solution.py:215
